TPU v7x, 32 devices: a whole 2x2x4 slice. The times are simulated.
32 devices in a mesh: ctx: 8 (over y, x, core), tp: 4 (over z).
Axes of the slice: x: 2, y: 2, z: 4, core: 2. Of those that a mesh axis runs over, the one named last changes fastest.
Arguments:
- hidden_in: bfloat16 [131072, 1536], P('ctx', 'tp'), may hold values from -6 to 6
- fac_inner: bfloat16 [512, 512], replicated, may hold values from -0.25 to 0.25
- fac_outer: bfloat16 [256, 256], replicated, may hold values from -0.375 to 0.375
- inv_outer: bfloat16 [256, 256], replicated, may hold values from -0.375 to 0.375
- inv_inner: bfloat16 [512, 512], replicated, may hold values from -0.25 to 0.25
- kernel_freq: bfloat16 [256, 512, 1536], P(None, 'ctx', 'tp'), may hold values from -6 to 6
- gate_blocks: bfloat16 [1536, 384], P('tp'), may hold values from -0.3125 to 0.3125
- mix_first: bfloat16 [1536, 384], P('tp'), may hold values from -0.3125 to 0.3125
- mix_second: bfloat16 [1536, 384], P('tp'), may hold values from -0.3125 to 0.3125
- upstream: bfloat16 [131072, 1536], P('ctx', 'tp'), may hold values from -6 to 6
Outputs:
- layer_out: bfloat16 [131072, 1536], P('ctx', 'tp')
- grad_input: bfloat16 [131072, 1536], P('ctx', 'tp')
- grad_kernel: float32 [256, 512, 1536], P(None, 'ctx', 'tp')
- grad_gate: float32 [1536, 384], P('tp', 'ctx')
- grad_first: float32 [1536, 384], P('tp', 'ctx')
- grad_second: float32 [1536, 384], P('tp', 'ctx')
All inputs are finite; a program needn't handle non-finite values.
Results may differ from a plain program's by a relative error of at most 0.015.
Values may be sent and summed in bfloat16 or wider, within the bound.
A program may use at most 384 MiB of HBM per device.

v0:
```python
import math

import jax
import jax.numpy as jnp
from jax import lax
from jax.sharding import PartitionSpec as P


def gelu_exact(values):
    return jax.nn.gelu(values, approximate=False)


def token_contract(left, right):
    return lax.dot_general(
        left, right, (((0,), (0,)), ((), ())), preferred_element_type=jnp.float32
    )


def right_transposed(left, right):
    return lax.dot_general(
        left, right, (((1,), (1,)), ((), ())), preferred_element_type=jnp.float32
    )


def spectral_return(cube):
    return lax.all_to_all(cube, "ctx", split_axis=0, concat_axis=1, tiled=True)


def regroup(matrix):
    result = lax.all_to_all(matrix, "tp", split_axis=1, concat_axis=1, tiled=True)
    return result


def local(
    hidden_in,
    fac_inner,
    fac_outer,
    inv_outer,
    inv_inner,
    kernel_freq,
    gate_blocks,
    mix_first,
    mix_second,
    upstream,
):
    tok_rows, local_width = hidden_in.shape
    inner_len = fac_inner.shape[0]
    local_outer = tok_rows // inner_len
    group_count = lax.axis_size("tp")
    piece_width = local_width // group_count
    cube_input = hidden_in.reshape(local_outer, inner_len, local_width)
    row_mixed = jnp.einsum(
        "abc,be->aec", cube_input, fac_inner, preferred_element_type=jnp.float32
    ).astype(jnp.bfloat16)
    columns = lax.all_to_all(row_mixed, "ctx", split_axis=1, concat_axis=0, tiled=True)
    spectrum = jnp.einsum("aec,af->fec", columns, fac_outer, preferred_element_type=jnp.float32)
    kernel_wide = kernel_freq.astype(jnp.float32)
    filtered = (spectrum * kernel_wide).astype(jnp.bfloat16)
    back_mixed = jnp.einsum(
        "fec,fg->gec", filtered, inv_outer, preferred_element_type=jnp.float32
    ).astype(jnp.bfloat16)
    returned = spectral_return(back_mixed)
    conv_flat = jnp.einsum(
        "aec,eb->abc", returned, inv_inner, preferred_element_type=jnp.float32
    ).reshape(tok_rows, local_width)
    gate_open = jax.nn.sigmoid(jnp.dot(hidden_in, gate_blocks, preferred_element_type=jnp.float32))
    mixed = (hidden_in.astype(jnp.float32) + gate_open * conv_flat).astype(jnp.bfloat16)
    first_out = jnp.dot(mixed, mix_first, preferred_element_type=jnp.float32).astype(jnp.bfloat16)
    shuffled = regroup(first_out)
    second_rows = (
        mix_second.reshape(piece_width, group_count, local_width)
        .transpose(1, 0, 2)
        .reshape(local_width, local_width)
    )
    second_local = (
        second_rows.reshape(local_width, piece_width, group_count)
        .transpose(0, 2, 1)
        .reshape(local_width, local_width)
    )
    second_out = jnp.dot(shuffled, second_local, preferred_element_type=jnp.float32).astype(
        jnp.bfloat16
    )
    merged = regroup(second_out)
    merged_wide = merged.astype(jnp.float32)
    layer_out = (mixed.astype(jnp.float32) + gelu_exact(merged_wide)).astype(jnp.bfloat16)
    unused, pull = jax.vjp(gelu_exact, merged_wide)
    grad_merged = pull(upstream.astype(jnp.float32))[0].astype(jnp.bfloat16)
    grad_second_out = regroup(grad_merged)
    grad_second_local = token_contract(shuffled, grad_second_out)
    grad_shuffled = right_transposed(grad_second_out, second_local).astype(jnp.bfloat16)
    grad_first_out = regroup(grad_shuffled)
    grad_first = token_contract(mixed, grad_first_out)
    grad_mixed = upstream.astype(jnp.float32) + right_transposed(grad_first_out, mix_first)
    grad_conv = (grad_mixed * gate_open).astype(jnp.bfloat16)
    grad_gate_pre = (grad_mixed * conv_flat * gate_open * (1.0 - gate_open)).astype(jnp.bfloat16)
    grad_gate = token_contract(hidden_in, grad_gate_pre)
    gate_back = right_transposed(grad_gate_pre, gate_blocks)
    grad_back = jnp.einsum(
        "abc,eb->aec",
        grad_conv.reshape(local_outer, inner_len, local_width),
        inv_inner,
        preferred_element_type=jnp.float32,
    ).astype(jnp.bfloat16)
    grad_columns = lax.all_to_all(grad_back, "ctx", split_axis=1, concat_axis=0, tiled=True)
    grad_filtered = jnp.einsum(
        "gec,fg->fec", grad_columns, inv_outer, preferred_element_type=jnp.float32
    )
    grad_kernel = grad_filtered * spectrum
    grad_spectrum = (grad_filtered * kernel_wide).astype(jnp.bfloat16)
    grad_row = jnp.einsum(
        "fec,af->aec", grad_spectrum, fac_outer, preferred_element_type=jnp.float32
    ).astype(jnp.bfloat16)
    grad_cube = spectral_return(grad_row)
    conv_back = jnp.einsum(
        "aec,be->abc", grad_cube, fac_inner, preferred_element_type=jnp.float32
    ).reshape(tok_rows, local_width)
    grad_input = (grad_mixed + gate_back + conv_back).astype(jnp.bfloat16)
    second_unrow = (
        grad_second_local.reshape(group_count, piece_width, local_width)
        .transpose(1, 0, 2)
        .reshape(local_width, local_width)
    )
    grad_second = (
        second_unrow.reshape(local_width, group_count, piece_width)
        .transpose(0, 2, 1)
        .reshape(local_width, local_width)
    )
    loss_scale = 1.0 / math.sqrt(tok_rows * lax.axis_size("ctx"))
    summed = (
        lax.psum_scatter(grad_gate * loss_scale, "ctx", scatter_dimension=1, tiled=True),
        lax.psum_scatter(grad_first * loss_scale, "ctx", scatter_dimension=1, tiled=True),
        lax.psum_scatter(grad_second * loss_scale, "ctx", scatter_dimension=1, tiled=True),
    )
    return (layer_out, grad_input, grad_kernel, summed[0], summed[1], summed[2])


def solution(mesh):
    placed = (
        P("ctx", "tp"),
        P(),
        P(),
        P(),
        P(),
        P(None, "ctx", "tp"),
        P("tp", None),
        P("tp", None),
        P("tp", None),
        P("ctx", "tp"),
    )
    return jax.shard_map(
        local,
        mesh=mesh,
        in_specs=placed,
        out_specs=(
            P("ctx", "tp"),
            P("ctx", "tp"),
            P(None, "ctx", "tp"),
            P("tp", "ctx"),
            P("tp", "ctx"),
            P("tp", "ctx"),
        ),
        check_vma=False,
    )
```

profile of v0, /device:TPU:0, one launch (start us, length us, event | category | flops | bytes accessed | tf_op | source)
XLA Modules:
  0.0 2314.3 jit_solution(975420884595020517)
XLA Ops:
  7.2 9.9 convert_bitcast_fusion.3
  17.1 34.4 %copy.130 = bf16[32,512,384]{2,0,1:T(8,128)(2,1)} copy(bf16[32,512,384]{2,1,0:T(8,128)(2,1)S(1)} %convert_bitcast_fusion.3) | data formatting | bytes 25165824 | tf_op jit(solution)/shard_map/convert_element_type | solution.py:54
  51.5 5.3 all-to-all-start
  56.9 17.4 copy.134
  74.3 122.2 %all-to-all-done = bf16[32,512,384]{2,0,1:T(8,128)(2,1)} async-done(((bf16[32,512,384]{2,0,1:T(8,128)(2,1)}), bf16[32,512,384]{2,0,1:T(8,128)(2,1)}, u32[]{:S(2)}, u32[]{:S(2)}) %all-to-all-start) | async-done | bytes 12582944 | tf_op jit(solution)/shard_map/all_to_all | solution.py:55
  196.5 13.6 copy.132
  210.2 39.5 %fusion.30 = f32[64,384,256]{2,1,0:T(8,128)} fusion(bf16[256,64,384]{2,1,0:T(8,128)(2,1)} %bitcast.141, bf16[256,256]{1,0:T(8,128)(2,1)S(1)} %copy-done.5), kind=kOutput, calls=%fused_computation.53 | convolution fusion | flops 3221225472 | bytes 37879808 | tf_op jit(solution)/shard_map/aec,af->fec/dot_general | solution.py:56
  249.7 18.1 convert_bitcast_fusion.2
  267.8 16.8 copy.135
  284.6 142.9 %all_to_all.117 = bf16[256,64,384]{2,1,0:T(8,128)(2,1)S(1)} all-to-all(bf16[256,64,384]{2,1,0:T(8,128)(2,1)} %copy.135), channel_id=1, replica_groups=mesh['ctx'=8,'tp'=4] {'ctx'}, dimensions={0} | all-to-all | bytes 25165824 | tf_op jit(solution)/shard_map/all_to_all | solution.py:26
  427.5 3.1 copy.136
  430.6 11.8 convolution_bitcast_fusion.1
  442.4 24.7 %copy.138 = f32[32,512,384]{2,1,0:T(8,128)} copy(f32[32,512,384]{1,2,0:T(8,128)} %convolution_bitcast_fusion.1) | data formatting | bytes 50331648 | tf_op jit(solution)/shard_map/aec,eb->abc/transpose | solution.py:63
  467.1 37.7 %fusion.13 = (bf16[16384,384]{1,0:T(8,128)(2,1)}, f32[16384,384]{1,0:T(8,128)}) fusion(f32[32,512,384]{2,1,0:T(8,128)} %copy.138, bf16[16384,384]{1,0:T(8,128)(2,1)} %param.10, bf16[384,384]{1,0:T(8,128)(2,1)S(1)} %copy-done.9), kind=kOutput, calls=%fused_computation.26 | convolution fusion | flops 4875878400 | bytes 75792384 | tf_op jit(solution)/shard_map/dot_general | solution.py:66
  504.8 12.5 convolution_convert_fusion
  517.3 6.8 all-to-all-start.2
  524.9 272.6 %all-to-all-done.2 = bf16[16384,4,96]{0,2,1:T(8,128)(2,1)} async-done(((bf16[16384,4,96]{0,2,1:T(8,128)(2,1)}), bf16[16384,4,96]{0,2,1:T(8,128)(2,1)}, u32[]{:S(2)}, u32[]{:S(2)}) %all-to-all-start.2) | async-done | bytes 12582944 | tf_op jit(solution)/shard_map/all_to_all | solution.py:30
  797.5 11.5 convolution_convert_fusion.1
  809.0 275.4 %all_to_all.118 = bf16[16384,4,96]{0,2,1:T(8,128)(2,1)S(1)} all-to-all(bf16[16384,4,96]{0,2,1:T(8,128)(2,1)S(1)} %bitcast.143), channel_id=1, replica_groups=mesh['ctx'=8,'tp'=4] {'tp'}, dimensions={1} | all-to-all | bytes 25165824 | tf_op jit(solution)/shard_map/all_to_all | solution.py:30
  1084.4 16.7 fusion.2
  1101.1 24.7 %copy.141 = f32[16384,384]{1,0:T(8,128)} copy(f32[16384,384]{0,1:T(8,128)} %bitcast.140) | data formatting | bytes 50331648 | tf_op jit(solution)/shard_map/mul | solution.py:10
  1125.8 24.7 %copy.146 = f32[16384,384]{1,0:T(8,128)} copy(f32[16384,384]{0,1:T(8,128)} %bitcast.139) | data formatting | bytes 50331648 | tf_op jit(solution)/shard_map/mul | solution.py:10
  1150.5 61.9 %fusion.9 = (bf16[16384,384]{1,0:T(8,128)(2,1)}, f32[16384,384]{1,0:T(8,128)}) fusion(f32[16384,384]{1,0:T(8,128)} %copy.146, bf16[16384,384]{1,0:T(8,128)(2,1)} %param.19, f32[16384,384]{1,0:T(8,128)} %copy.141), kind=kLoop, calls=%fused_computation.17 | loop fusion | flops 440401920 | bytes 100663296 | tf_op jit(solution)/shard_map/convert_element_type | solution.py:87
  1212.4 16.7 copy.148
  1229.1 276.4 %all_to_all.119 = bf16[16384,4,96]{0,2,1:T(8,128)(2,1)S(1)} all-to-all(bf16[16384,4,96]{0,2,1:T(8,128)(2,1)} %bitcast.152), channel_id=1, replica_groups=mesh['ctx'=8,'tp'=4] {'tp'}, dimensions={1} | all-to-all | bytes 25165824 | tf_op jit(solution)/shard_map/all_to_all | solution.py:30
  1505.5 9.9 bitcast_convert_fusion
  1515.3 281.5 %all_to_all.120 = bf16[16384,4,96]{0,2,1:T(8,128)(2,1)} all-to-all(bf16[16384,4,96]{0,2,1:T(8,128)(2,1)} %bitcast.150), channel_id=1, replica_groups=mesh['ctx'=8,'tp'=4] {'tp'}, dimensions={1} | all-to-all | bytes 25165824 | tf_op jit(solution)/shard_map/all_to_all | solution.py:30
  1796.9 43.1 %fusion.16 = (bf16[16384,384]{1,0:T(8,128)(2,1)}, bf16[16384,384]{1,0:T(8,128)(2,1)}, f32[16384,384]{1,0:T(8,128)}) fusion(f32[16384,384]{1,0:T(8,128)} %get-tuple-element.43, f32[32,512,384]{2,1,0:T(8,128)} %copy.138, bf16[16384,384]{0,1:T(8,128)(2,1)} %bitcast.144, bf16[384,384]{1,0:T(8,128)(2,1)S(1)} %copy-done.3, bf16[16384,384]{1,0:T(8,128)(2,1)} %param.19), kind=kOutput, calls=%fused_computation.29 | convolution fusion | flops 4888461312 | bytes 126124032 | tf_op jit(solution)/shard_map/dot_general | solution.py:20
  1839.9 14.3 convert_bitcast_fusion.1
  1854.2 17.3 copy.151
  1871.5 143.0 %all_to_all.121 = bf16[32,512,384]{2,0,1:T(8,128)(2,1)S(1)} all-to-all(bf16[32,512,384]{2,0,1:T(8,128)(2,1)} %copy.151), channel_id=1, replica_groups=mesh['ctx'=8,'tp'=4] {'ctx'}, dimensions={1} | all-to-all | bytes 25165824 | tf_op jit(solution)/shard_map/all_to_all | solution.py:104
  2014.5 6.8 copy.153
  2021.4 31.5 %bitcast_multiply_fusion = (f32[256,64,384]{0,2,1:T(8,128)}, f32[64,384,256]{2,1,0:T(8,128)}) fusion(f32[64,384,256]{2,1,0:T(8,128)} %fusion.30, bf16[256,256]{1,0:T(8,128)(2,1)S(1)} %copy-done.8, bf16[256,64,384]{2,1,0:T(8,128)(2,1)} %bitcast.142), kind=kOutput, calls=%fused_computation.21 | convolution fusion | flops 3227516928 | bytes 88211456 | tf_op jit(solution)/shard_map/gec,fg->fec/dot_general | solution.py:105
  2052.9 18.2 convert_bitcast_fusion
  2071.0 16.5 copy.155
  2087.5 5.5 all-to-all-start.7
  2093.1 25.0 %add_convert_fusion = bf16[16384,384]{1,0:T(8,128)(2,1)} fusion(f32[16384,384]{1,0:T(8,128)} %copy.146, f32[16384,384]{1,0:T(8,128)} %get-tuple-element.37, bf16[16384,384]{1,0:T(8,128)(2,1)} %get-tuple-element.42), kind=kLoop, calls=%fused_computation.31 | loop fusion | flops 25165824 | bytes 75497472 | tf_op jit(solution)/shard_map/convert_element_type | solution.py:85
  2118.1 17.3 fusion.39
  2136.7 1.0 mul.113
  2137.8 17.3 convolution_multiply_fusion
  2155.1 1.0 copy.175
  2156.3 12.9 fusion.42
  2169.1 25.0 %copy.163 = f32[256,64,384]{2,1,0:T(8,128)} copy(f32[256,64,384]{0,2,1:T(8,128)} %get-tuple-element.45) | data formatting | bytes 50331648
  2194.1 41.9 %all-to-all-done.7 = bf16[256,64,384]{2,1,0:T(8,128)(2,1)} async-done(((bf16[256,64,384]{2,1,0:T(8,128)(2,1)}), bf16[256,64,384]{2,1,0:T(8,128)(2,1)}, u32[]{:S(2)}, u32[]{:S(2)}) %all-to-all-start.7) | async-done | bytes 12582944 | tf_op jit(solution)/shard_map/all_to_all | solution.py:26
  2236.0 7.2 copy.156
  2243.2 12.1 convolution_bitcast_fusion
  2255.3 24.7 %copy.158 = f32[32,512,384]{2,1,0:T(8,128)} copy(f32[32,512,384]{1,2,0:T(8,128)} %convolution_bitcast_fusion) | data formatting | bytes 50331648 | tf_op jit(solution)/shard_map/aec,be->abc/transpose | solution.py:114
  2280.0 27.3 %fusion.11 = bf16[16384,384]{1,0:T(8,128)(2,1)} fusion(f32[32,512,384]{2,1,0:T(8,128)} %copy.158, f32[16384,384]{1,0:T(8,128)} %get-tuple-element.44, bf16[16384,384]{1,0:T(8,128)(2,1)} %get-tuple-element.38, bf16[384,384]{1,0:T(8,128)(2,1)S(1)} %copy-done.10), kind=kOutput, calls=%fused_computation.20 | convolution fusion | flops 4850712576 | bytes 75792384 | tf_op jit(solution)/shard_map/dot_general | solution.py:20
  (40 shorter events, 2.3 us)
Async XLA Ops:
  7.2 423.4 %copy-start = (bf16[512,512]{1,0:T(8,128)(2,1)S(1)}, bf16[512,512]{1,0:T(8,128)(2,1)}, u32[]{:S(2)}) copy-start(bf16[512,512]{1,0:T(8,128)(2,1)} %param.14) | copy-start | bytes 1572868
  51.5 145.0 %all-to-all-start = ((bf16[32,512,384]{2,0,1:T(8,128)(2,1)}), bf16[32,512,384]{2,0,1:T(8,128)(2,1)}, u32[]{:S(2)}, u32[]{:S(2)}) async-start(bf16[32,512,384]{2,0,1:T(8,128)(2,1)} %copy.130), calls=%async_computation | async-start | bytes 25165824 | tf_op jit(solution)/shard_map/all_to_all | solution.py:55
  56.8 153.3 %copy-start.5 = (bf16[256,256]{1,0:T(8,128)(2,1)S(1)}, bf16[256,256]{1,0:T(8,128)(2,1)}, u32[]{:S(2)}) copy-start(bf16[256,256]{1,0:T(8,128)(2,1)} %param.12) | copy-start | bytes 393220
  210.1 39.5 %copy-start.7 = (bf16[256,256]{1,0:T(8,128)(2,1)S(1)}, bf16[256,256]{1,0:T(8,128)(2,1)}, u32[]{:S(2)}) copy-start(bf16[256,256]{1,0:T(8,128)(2,1)} %param.13) | copy-start | bytes 393220
  442.4 24.7 %copy-start.9 = (bf16[384,384]{1,0:T(8,128)(2,1)S(1)}, bf16[384,384]{1,0:T(8,128)(2,1)}, u32[]{:S(2)}) copy-start(bf16[384,384]{1,0:T(8,128)(2,1)} %param.16) | copy-start | bytes 884740
  467.1 37.7 %copy-start.3 = (bf16[384,384]{1,0:T(8,128)(2,1)S(1)}, bf16[384,384]{1,0:T(8,128)(2,1)}, u32[]{:S(2)}) copy-start(bf16[384,384]{1,0:T(8,128)(2,1)} %param.17) | copy-start | bytes 884740
  504.8 19.3 copy-start.11
  517.3 280.2 %all-to-all-start.2 = ((bf16[16384,4,96]{0,2,1:T(8,128)(2,1)}), bf16[16384,4,96]{0,2,1:T(8,128)(2,1)}, u32[]{:S(2)}, u32[]{:S(2)}) async-start(bf16[16384,4,96]{0,2,1:T(8,128)(2,1)} %bitcast.146), calls=%async_computation.2 | async-start | bytes 25165824 | tf_op jit(solution)/shard_map/all_to_all | solution.py:30
  1505.5 291.4 %copy-start.2 = (bf16[16384,4,96]{0,2,1:T(8,128)(2,1)}, bf16[16384,4,96]{0,2,1:T(8,128)(2,1)S(1)}, u32[]{:S(2)}) copy-start(bf16[16384,4,96]{0,2,1:T(8,128)(2,1)S(1)} %all_to_all.119) | copy-start | bytes 37748740
  1871.5 149.9 %copy-start.8 = (bf16[256,256]{1,0:T(8,128)(2,1)S(1)}, bf16[256,256]{1,0:T(8,128)(2,1)}, u32[]{:S(2)}) copy-start(bf16[256,256]{1,0:T(8,128)(2,1)} %param.13) | copy-start | bytes 393220
  2021.4 31.5 %copy-start.6 = (bf16[256,256]{1,0:T(8,128)(2,1)S(1)}, bf16[256,256]{1,0:T(8,128)(2,1)}, u32[]{:S(2)}) copy-start(bf16[256,256]{1,0:T(8,128)(2,1)} %param.12) | copy-start | bytes 393220
  2087.5 148.5 %all-to-all-start.7 = ((bf16[256,64,384]{2,1,0:T(8,128)(2,1)}), bf16[256,64,384]{2,1,0:T(8,128)(2,1)}, u32[]{:S(2)}, u32[]{:S(2)}) async-start(bf16[256,64,384]{2,1,0:T(8,128)(2,1)} %copy.155), calls=%async_computation.7 | async-start | bytes 25165824 | tf_op jit(solution)/shard_map/all_to_all | solution.py:26
  2093.1 214.2 %reduce-scatter.8.cloned.1.call-start = ((), (), s32[]{:S(2)}) async-start(), calls=%async_computation.12 | async-start | bytes 663552 | tf_op jit(solution)/shard_map/reduce_scatter | solution.py:132
  2137.7 169.6 %reduce-scatter.10.cloned.1.call-start = ((), (), s32[]{:S(2)}) async-start(), calls=%async_computation.13 | async-start | bytes 663552
  2156.2 151.1 %reduce-scatter.6.cloned.1.call-start = ((), (), s32[]{:S(2)}) async-start(), calls=%async_computation.11 | async-start | bytes 663552 | tf_op jit(solution)/shard_map/reduce_scatter | solution.py:130
  2194.1 49.1 %copy-start.4 = (bf16[512,512]{1,0:T(8,128)(2,1)S(1)}, bf16[512,512]{1,0:T(8,128)(2,1)}, u32[]{:S(2)}) copy-start(bf16[512,512]{1,0:T(8,128)(2,1)} %param.11) | copy-start | bytes 1572868
  2255.3 24.7 %copy-start.10 = (bf16[384,384]{1,0:T(8,128)(2,1)S(1)}, bf16[384,384]{1,0:T(8,128)(2,1)}, u32[]{:S(2)}) copy-start(bf16[384,384]{1,0:T(8,128)(2,1)} %param.16) | copy-start | bytes 884740
  2280.0 27.3 %copy-start.1 = (bf16[512,512]{1,0:T(8,128)(2,1)S(1)}, bf16[512,512]{1,0:T(8,128)(2,1)}, u32[]{:S(2)}) copy-start(bf16[512,512]{1,0:T(8,128)(2,1)} %param.14) | copy-start | bytes 1572868
Sparse Core Ops, SparseCore 0:
  2137.9 38.1 reduce-scatter.7
  2179.8 59.7 reduce-scatter.9
  2243.2 34.3 reduce-scatter.5
where the time goes:
time: 2330 us; the launch traced here: 2310 us
  blocking collectives  1120 us (48%)
  waiting for transfers between devices  437 us (19%)
  matrix products  345 us (15%)
  local copies, waits for them, and re-layouts  278 us (12%)
  other arithmetic  104 us (4%)
    all_to_all x3, blocking collectives, regroup(): lax.all_to_all(matrix, 'tp', split_axis=1, concat_axis=1, tiled=True)  833 us
    all_to_all x1, waiting for transfers between devices, regroup(): lax.all_to_all(matrix, 'tp', split_axis=1, concat_axis=1, tiled=True)  273 us
    all_to_all x1, blocking collectives, local(): lax.all_to_all(grad_back, 'ctx', split_axis=1, concat_axis=0, tiled=True)  143 us
    all_to_all x1, blocking collectives, spectral_return(): return lax.all_to_all(cube, 'ctx', split_axis=0, concat_axis=1, tiled=True)  143 us
    all_to_all x1, waiting for transfers between devices, local(): lax.all_to_all(row_mixed, 'ctx', split_axis=1, concat_axis=0, tiled=True)  122 us
    dot_general x3, matrix products, right_transposed(): lax.dot_general(left, right, (((1,), (1,)), ((), ())), preferred_element_...  80.2 us
    convert_element_type x1, other arithmetic, local(): grad_merged = pull(upstream.astype(jnp.float32))[0].astype(jnp.bfloat16)  61.9 us
    mul x2, local copies, waits for them, and re-layouts, gelu_exact(): return jax.nn.gelu(values, approximate=False)  49.4 us
  transfers between devices with their start and end apart: 6, of which 3 were waited for; matrix products, arithmetic and copies ran while one was open for 8% of the time, Pallas kernels for 0%

commit v1 on v0

v1 whole, which is shorter than its diff:
```python
import math

import jax
import jax.numpy as jnp
from jax import lax
from jax.sharding import PartitionSpec as P

PARTS = 4


def gelu_exact(values):
    return jax.nn.gelu(values, approximate=False)


def token_contract(left, right):
    return lax.dot_general(
        left, right, (((0,), (0,)), ((), ())), preferred_element_type=jnp.float32
    )


def right_transposed(left, right):
    return lax.dot_general(
        left, right, (((1,), (1,)), ((), ())), preferred_element_type=jnp.float32
    )


def shifted(values, by):
    group_count = lax.axis_size("tp")
    pairs = [(at, (at + by) % group_count) for at in range(group_count)]
    return lax.ppermute(values, "tp", pairs)


def to_tokens(chunk):
    group_count = lax.axis_size("tp")
    here = lax.axis_index("tp")
    rows = chunk.shape[0] // group_count
    pieces = []
    for by in range(group_count):
        goal = lax.rem(here + by, group_count)
        piece = lax.dynamic_slice_in_dim(chunk, goal * rows, rows, 0)
        pieces.append(piece if by == 0 else shifted(piece, by))
    return jnp.concatenate(pieces, axis=1)


def to_channels(matrix):
    group_count = lax.axis_size("tp")
    here = lax.axis_index("tp")
    rows, width = matrix.shape[0], matrix.shape[1] // group_count
    result = jnp.zeros((rows * group_count, width), matrix.dtype)
    for by in range(group_count):
        piece = matrix[:, by * width : (by + 1) * width]
        if by:
            piece = shifted(piece, group_count - by)
        quarter = lax.rem(here + by, group_count)
        result = lax.dynamic_update_slice_in_dim(result, piece, quarter * rows, 0)
    return result


def turned(values, axis):
    group_count = lax.axis_size("tp")
    here = lax.axis_index("tp")
    blocks = [
        lax.dynamic_slice_in_dim(values, lax.rem(here - by + group_count, group_count), 1, axis)
        for by in range(group_count)
    ]
    return jnp.concatenate(blocks, axis=axis)


def spread_second(mix_second):
    width = mix_second.shape[0]
    group_count = lax.axis_size("tp")
    piece = width // group_count
    second_rows = (
        mix_second.reshape(piece, group_count, width).transpose(1, 0, 2).reshape(width, width)
    )
    second_local = (
        second_rows.reshape(width, piece, group_count).transpose(0, 2, 1).reshape(width, width)
    )
    blocks = lax.all_gather(second_local, "tp", axis=0, tiled=False)
    blocks = blocks.reshape(group_count, group_count, piece, group_count, piece)
    blocks = turned(turned(blocks, 1), 3)
    parts = []
    for k in range(group_count):
        gaps = ((0, 0), (0, 0), (0, 0), (k * piece, width - (k + 1) * piece))
        parts.append(jnp.pad(blocks[k], gaps))
    whole = group_count * width
    return jnp.concatenate(parts, axis=1).reshape(whole, whole)


def gather_second(full):
    group_count = lax.axis_size("tp")
    width = full.shape[0] // group_count
    piece = width // group_count
    cube = full.reshape(group_count, width, group_count, width)
    blocks = jnp.stack(
        [
            cube[:, k * piece : (k + 1) * piece, :, k * piece : (k + 1) * piece]
            for k in range(group_count)
        ]
    )
    blocks = turned(turned(blocks, 1), 3).reshape(group_count * width, width)
    local_sum = lax.psum_scatter(blocks, "tp", scatter_dimension=0, tiled=True)
    unrow = (
        local_sum.reshape(group_count, piece, width).transpose(1, 0, 2).reshape(width, width)
    )
    return unrow.reshape(width, group_count, piece).transpose(0, 2, 1).reshape(width, width)


def chunk_order(matrix, axis, parts):
    devices = lax.axis_size("ctx")
    moved = jnp.moveaxis(matrix, axis, 0)
    length, other = moved.shape
    rows = length // (devices * parts)
    moved = moved.reshape(devices, parts, rows, other).transpose(1, 0, 2, 3)
    return jnp.moveaxis(moved.reshape(length, other), 0, axis)


def local(
    hidden_in,
    fac_inner,
    fac_outer,
    inv_outer,
    inv_inner,
    kernel_freq,
    gate_blocks,
    mix_first,
    mix_second,
    upstream,
):
    tok_rows, local_width = hidden_in.shape
    inner_len = fac_inner.shape[0]
    outer_len = fac_outer.shape[0]
    local_outer = tok_rows // inner_len
    parts = min(PARTS, local_outer)
    part_outer = local_outer // parts
    part_rows = tok_rows // parts
    part_span = outer_len // parts

    def rows_of(matrix, part):
        return matrix[part * part_rows : (part + 1) * part_rows]

    second_full = spread_second(mix_second)
    inv_outer_parts = chunk_order(inv_outer, 1, parts)
    fac_outer_parts = chunk_order(fac_outer, 0, parts)

    up_tokens = [to_tokens(rows_of(upstream, part)) for part in range(parts)]

    cube_input = hidden_in.reshape(local_outer, inner_len, local_width)
    row_mixed = jnp.einsum(
        "abc,be->aec", cube_input, fac_inner, preferred_element_type=jnp.float32
    ).astype(jnp.bfloat16)
    columns = lax.all_to_all(row_mixed, "ctx", split_axis=1, concat_axis=0, tiled=True)
    spectrum = jnp.einsum("aec,af->fec", columns, fac_outer, preferred_element_type=jnp.float32)
    kernel_wide = kernel_freq.astype(jnp.float32)
    filtered = (spectrum * kernel_wide).astype(jnp.bfloat16)
    back_mixed = jnp.einsum(
        "fec,fg->gec", filtered, inv_outer_parts, preferred_element_type=jnp.float32
    ).astype(jnp.bfloat16)
    back_mixed, up_tokens = lax.optimization_barrier((back_mixed, up_tokens))

    gates, convs, mixes, firsts, mergeds = [], [], [], [], []
    slopes, grad_firsts = [], []
    for part in range(parts):
        returned = lax.all_to_all(
            back_mixed[part * part_span : (part + 1) * part_span],
            "ctx",
            split_axis=0,
            concat_axis=1,
            tiled=True,
        )
        conv_flat = jnp.einsum(
            "aec,eb->abc", returned, inv_inner, preferred_element_type=jnp.float32
        ).reshape(part_rows, local_width)
        tokens = rows_of(hidden_in, part)
        gate_open = jax.nn.sigmoid(jnp.dot(tokens, gate_blocks, preferred_element_type=jnp.float32))
        mixed = (tokens.astype(jnp.float32) + gate_open * conv_flat).astype(jnp.bfloat16)
        first_out = jnp.dot(mixed, mix_first, preferred_element_type=jnp.float32).astype(
            jnp.bfloat16
        )
        gates.append(gate_open)
        convs.append(conv_flat)
        mixes.append(mixed)
        firsts.append(to_tokens(first_out))
    for part in range(parts):
        merged = jnp.dot(firsts[part], second_full, preferred_element_type=jnp.float32).astype(
            jnp.bfloat16
        )
        unused, pull = jax.vjp(gelu_exact, merged.astype(jnp.float32))
        grad_merged = pull(up_tokens[part].astype(jnp.float32))[0].astype(jnp.bfloat16)
        grad_shuffled = right_transposed(grad_merged, second_full).astype(jnp.bfloat16)
        mergeds.append(merged)
        slopes.append(grad_merged)
        grad_firsts.append(to_channels(grad_shuffled))

    grad_first = 0.0
    grad_gate = 0.0
    bases, grad_columns = [], []
    for part in range(parts):
        grad_first = grad_first + token_contract(mixes[part], grad_firsts[part])
        grad_mixed = rows_of(upstream, part).astype(jnp.float32) + right_transposed(
            grad_firsts[part], mix_first
        )
        gate_open, conv_flat = gates[part], convs[part]
        grad_conv = (grad_mixed * gate_open).astype(jnp.bfloat16)
        grad_gate_pre = (grad_mixed * conv_flat * gate_open * (1.0 - gate_open)).astype(
            jnp.bfloat16
        )
        grad_gate = grad_gate + token_contract(rows_of(hidden_in, part), grad_gate_pre)
        bases.append(grad_mixed + right_transposed(grad_gate_pre, gate_blocks))
        grad_back = jnp.einsum(
            "abc,eb->aec",
            grad_conv.reshape(part_outer, inner_len, local_width),
            inv_inner,
            preferred_element_type=jnp.float32,
        ).astype(jnp.bfloat16)
        grad_columns.append(
            lax.all_to_all(grad_back, "ctx", split_axis=1, concat_axis=0, tiled=True)
        )
    mergeds, tied = lax.optimization_barrier((mergeds, grad_firsts[-1]))
    layer_out = jnp.concatenate(
        [
            (
                mixes[part].astype(jnp.float32)
                + gelu_exact(to_channels(mergeds[part]).astype(jnp.float32))
            ).astype(jnp.bfloat16)
            for part in range(parts)
        ]
    )
    grad_filtered = jnp.einsum(
        "gec,fg->fec",
        jnp.concatenate(grad_columns),
        inv_outer_parts,
        preferred_element_type=jnp.float32,
    )
    grad_kernel = grad_filtered * spectrum
    grad_spectrum = (grad_filtered * kernel_wide).astype(jnp.bfloat16)
    grad_row = jnp.einsum(
        "fec,af->aec", grad_spectrum, fac_outer_parts, preferred_element_type=jnp.float32
    ).astype(jnp.bfloat16)
    inputs = []
    for part in range(parts):
        grad_cube = lax.all_to_all(
            grad_row[part * part_span : (part + 1) * part_span],
            "ctx",
            split_axis=0,
            concat_axis=1,
            tiled=True,
        )
        conv_back = jnp.einsum(
            "aec,be->abc", grad_cube, fac_inner, preferred_element_type=jnp.float32
        ).reshape(part_rows, local_width)
        inputs.append((bases[part] + conv_back).astype(jnp.bfloat16))
    grad_input = jnp.concatenate(inputs)
    second_product = 0.0
    for part in range(parts):
        second_product = second_product + token_contract(firsts[part], slopes[part])
    grad_second = gather_second(second_product)
    loss_scale = 1.0 / math.sqrt(tok_rows * lax.axis_size("ctx"))
    summed = (
        lax.psum_scatter(grad_gate * loss_scale, "ctx", scatter_dimension=1, tiled=True),
        lax.psum_scatter(grad_first * loss_scale, "ctx", scatter_dimension=1, tiled=True),
        lax.psum_scatter(grad_second * loss_scale, "ctx", scatter_dimension=1, tiled=True),
    )
    return (layer_out, grad_input, grad_kernel, summed[0], summed[1], summed[2])


def solution(mesh):
    placed = (
        P("ctx", "tp"),
        P(),
        P(),
        P(),
        P(),
        P(None, "ctx", "tp"),
        P("tp", None),
        P("tp", None),
        P("tp", None),
        P("ctx", "tp"),
    )
    return jax.shard_map(
        local,
        mesh=mesh,
        in_specs=placed,
        out_specs=(
            P("ctx", "tp"),
            P("ctx", "tp"),
            P(None, "ctx", "tp"),
            P("tp", "ctx"),
            P("tp", "ctx"),
            P("tp", "ctx"),
        ),
        check_vma=False,
    )
```

time: 2330 us -> 2240 us (0.961)
  blocking collectives: 1120 us -> 0 us
  starting transfers between devices: 17.8 us -> 513 us
  other arithmetic: 104 us -> 271 us
  waiting for transfers between devices: 437 us -> 603 us
  local copies, waits for them, and re-layouts: 278 us -> 412 us
  matrix products: 345 us -> 416 us
    all_to_all x5 -> x0, blocking collectives: 1120 us -> none  [the longest x3 833 us: regroup(): lax.all_to_all(matrix, 'tp', split_axis=1, concat_axis=1, tiled=True)]
    ppermute x0 -> x48, waiting for transfers between devices: none -> 487 us  [shifted(): return lax.ppermute(values, 'tp', pairs)]
    ppermute x0 -> x48, starting transfers between devices: none -> 453 us  [shifted(): return lax.ppermute(values, 'tp', pairs)]
    all_to_all x2 -> x12, waiting for transfers between devices: 315 us -> 116 us  [the longest x4 54.5 us: local(): lax.all_to_all(grad_row[part * part_span:(part + 1) * part_span], 'ctx',...]
    concatenate x0 -> x11, other arithmetic: none -> 143 us  [the longest x1 72.4 us: local(): grad_input = jnp.concatenate(inputs)]
    all_to_all x1, waiting for transfers between devices: 122 us -> 0.01 us  [local(): lax.all_to_all(row_mixed, 'ctx', split_axis=1, concat_axis=0, tiled=True)]
    slice x0 -> x19, local copies, waits for them, and re-layouts: none -> 98.9 us  [the longest x5 53.1 us: local(): back_mixed[part * part_span:(part + 1) * part_span]]
    mul x2 -> x0, local copies, waits for them, and re-layouts: 49.4 us -> none  [gelu_exact(): return jax.nn.gelu(values, approximate=False)]
  transfers between devices with their start and end apart: 6 -> 66, of which waited for: 3 -> 25; matrix products, arithmetic and copies ran while one was open for 8% -> 36% of each run, Pallas kernels for 0% -> 0%
where the time goes in v1:
time: 2240 us; the launch traced here: 2230 us
  waiting for transfers between devices  603 us (27%)
  starting transfers between devices  513 us (23%)
  matrix products  416 us (19%)
  local copies, waits for them, and re-layouts  412 us (18%)
  other arithmetic  271 us (12%)
    ppermute x48, waiting for transfers between devices, shifted(): return lax.ppermute(values, 'tp', pairs)  487 us
    ppermute x48, starting transfers between devices, shifted(): return lax.ppermute(values, 'tp', pairs)  453 us
    dot_general x12, matrix products, right_transposed(): lax.dot_general(left, right, (((1,), (1,)), ((), ())), preferred_element_...  95 us
    concatenate x1, other arithmetic, local(): grad_input = jnp.concatenate(inputs)  72.4 us
    dot_general x12, matrix products, token_contract(): lax.dot_general(left, right, (((0,), (0,)), ((), ())), preferred_element_...  71.6 us
    convert_element_type x4, other arithmetic, local(): layer_out = jnp.concatenate([(mixes[part].astype(jnp.float32) + gelu_exac...  64.8 us
    convert_element_type x4, other arithmetic, local(): pull(up_tokens[part].astype(jnp.float32))[0].astype(jnp.bfloat16)  60.5 us
    unnamed x135, local copies, waits for them, and re-layouts  55.3 us
  transfers between devices with their start and end apart: 66, of which 25 were waited for; matrix products, arithmetic and copies ran while one was open for 36% of the time, Pallas kernels for 0%

profile of v1, /device:TPU:0, one launch (start us, length us, event | category | flops | bytes accessed | tf_op | source)
XLA Modules:
  0.0 2229.8 jit_solution(16883225286985240686)
XLA Ops:
  17.1 34.4 %copy.242 = bf16[32,512,384]{2,0,1:T(8,128)(2,1)} copy(bf16[32,512,384]{2,1,0:T(8,128)(2,1)S(1)} %convert_bitcast_fusion.2) | data formatting | bytes 25165824 | tf_op jit(solution)/shard_map/convert_element_type | solution.py:151
  88.3 31.5 %collective-permute-done.1 = bf16[1024,384]{1,0:T(8,128)(2,1)} collective-permute-done((bf16[1024,384]{1,0:T(8,128)(2,1)S(1)}, bf16[1024,384]{1,0:T(8,128)(2,1)}, u32[]{:S(2)}, u32[]{:S(2)}) %collective-permute-start.1) | collective-permute-done | bytes 786464 | tf_op jit(solution)/shard_map/ppermute | solution.py:30
  119.9 49.2 %collective-permute-start.6 = (bf16[1024,384]{1,0:T(8,128)(2,1)}, bf16[1024,384]{1,0:T(8,128)(2,1)}, u32[]{:S(2)}, u32[]{:S(2)}) collective-permute-start(bf16[1024,384]{1,0:T(8,128)(2,1)} %get-tuple-element.145), channel_id=1, source_target_pairs={{0,1},{1,2},{2,3},{3,0},{4,5},{5,6},{6,7},{7,4},{8,9},{9,10},{10,1... | collective-permute-start | bytes 2359304 | tf_op jit(solution)/shard_map/ppermute | solution.py:30
  175.1 17.4 copy.246
  192.7 28.1 %collective-permute-done.4 = bf16[1024,384]{1,0:T(8,128)(2,1)} collective-permute-done((bf16[1024,384]{1,0:T(8,128)(2,1)}, bf16[1024,384]{1,0:T(8,128)(2,1)}, u32[]{:S(2)}, u32[]{:S(2)}) %collective-permute-start.4) | collective-permute-done | bytes 786464 | tf_op jit(solution)/shard_map/ppermute | solution.py:30
  220.7 20.6 collective-permute-start.10
  241.3 23.7 %collective-permute-start.11 = (bf16[1024,384]{1,0:T(8,128)(2,1)}, bf16[1024,384]{1,0:T(8,128)(2,1)S(1)}, u32[]{:S(2)}, u32[]{:S(2)}) collective-permute-start(bf16[1024,384]{1,0:T(8,128)(2,1)} %get-tuple-element.139), channel_id=1, source_target_pairs={{0,3},{1,0},{2,1},{3,2},{4,7},{5,4},{6,5},{7,6},{8,11},{9,8},{10,9... | collective-permute-start | bytes 2359304 | tf_op jit(solution)/shard_map/ppermute | solution.py:30
  265.0 22.5 %collective-permute-start.9 = (bf16[1024,384]{1,0:T(8,128)(2,1)}, bf16[1024,384]{1,0:T(8,128)(2,1)S(1)}, u32[]{:S(2)}, u32[]{:S(2)}) collective-permute-start(bf16[1024,384]{1,0:T(8,128)(2,1)} %get-tuple-element.141), channel_id=1, source_target_pairs={{0,1},{1,2},{2,3},{3,0},{4,5},{5,6},{6,7},{7,4},{8,9},{9,10},{10,1... | collective-permute-start | bytes 2359304 | tf_op jit(solution)/shard_map/ppermute | solution.py:30
  296.6 25.2 %collective-permute-done.10 = bf16[1024,384]{1,0:T(8,128)(2,1)S(1)} collective-permute-done((bf16[1024,384]{1,0:T(8,128)(2,1)}, bf16[1024,384]{1,0:T(8,128)(2,1)S(1)}, u32[]{:S(2)}, u32[]{:S(2)}) %collective-permute-start.10) | collective-permute-done | bytes 786464 | tf_op jit(solution)/shard_map/ppermute | solution.py:30
  337.0 37.5 %fusion.14 = f32[64,384,256]{2,1,0:T(8,128)} fusion(bf16[256,64,384]{2,1,0:T(8,128)(2,1)} %bitcast.320, bf16[256,256]{1,0:T(8,128)(2,1)S(1)} %copy-done.42), kind=kOutput, calls=%fused_computation.21 | convolution fusion | flops 3221225472 | bytes 37879808 | tf_op jit(solution)/shard_map/aec,af->fec/dot_general | solution.py:153
  374.5 18.2 convert_bitcast_fusion.1
  392.6 21.5 fusion.383
  434.4 30.0 %all-to-all-done.1 = bf16[64,64,384]{2,1,0:T(8,128)(2,1)} async-done(((bf16[64,64,384]{2,1,0:T(8,128)(2,1)}), bf16[64,64,384]{2,1,0:T(8,128)(2,1)}, u32[]{:S(2)}, u32[]{:S(2)}) %all-to-all-start.1) | async-done | bytes 3145760 | tf_op jit(solution)/shard_map/all_to_all | solution.py:164
  486.4 20.3 all-to-all-done.2
  554.1 32.1 %fusion.323 = bf16[4,384,4,384]{3,2,1,0:T(4,128)(2,1)S(1)} fusion(bf16[4,96,4,96]{3,2,1,0:T(4,128)(2,1)S(1)} %get-tuple-element.155, bf16[4,96,4,96]{3,2,1,0:T(4,128)(2,1)S(1)} %get-tuple-element.156, bf16[4,96,4,96]{3,2,1,0:T(4,128)(2,1)S(1)} %get-tuple-element.157, bf16[4,96,4,96]{3,2,1,0:T(4,128)(2,1)S(1)} %get-tuple-element.154), kind=kLoop, calls=%fused_computation.392 | loop fusion | flops 47185920 | bytes 5898240 | tf_op jit(solution)/shard_map/concatenate | solution.py:87
  643.2 26.9 %fusion.303 = (bf16[4096,384]{1,0:T(8,128)(2,1)}, bf16[4096,384]{1,0:T(8,128)(2,1)}, bf16[4096,384]{1,0:T(8,128)(2,1)}, bf16[4096,384]{1,0:T(8,128)(2,1)}, f32[4096,384]{1,0:T(8,128)}) fusion(f32[8,512,384]{2,1,0:T(8,128)} %copy.267, bf16[16384,384]{1,0:T(8,128)(2,1)} %param.10, f32[4096,384]{1,0:T(8,128)} %add_divide_fusion.2, f32[8,512,384]{2,1,0:T(8,128)} %copy.259, ...), kind=kOutput, calls=%fused_computation.350 | convolution fusion | flops 1237843968 | bytes 78938112 | tf_op jit(solution)/shard_map/dot_general | solution.py:175
  674.5 17.4 collective-permute-start.15
  712.2 32.8 %collective-permute-done.16 = bf16[1024,384]{0,1:T(8,128)(2,1)S(1)} collective-permute-done((bf16[1024,384]{0,1:T(8,128)(2,1)S(1)}, bf16[1024,384]{0,1:T(8,128)(2,1)S(1)}, u32[]{:S(2)}, u32[]{:S(2)}) %collective-permute-start.16) | collective-permute-done | bytes 786464 | tf_op jit(solution)/shard_map/ppermute | solution.py:30
  745.0 19.3 collective-permute-start.20
  795.6 66.6 %collective-permute-start.21 = (bf16[1024,384]{0,1:T(8,128)(2,1)S(1)}, bf16[1024,384]{0,1:T(8,128)(2,1)S(1)}, u32[]{:S(2)}, u32[]{:S(2)}) collective-permute-start(bf16[1024,384]{0,1:T(8,128)(2,1)S(1)} %get-tuple-element.125), channel_id=1, source_target_pairs={{0,1},{1,2},{2,3},{3,0},{4,5},{5,6},{6,7},{7,4},{8,9},{9,10},{10,1... | collective-permute-start | bytes 2359304 | tf_op jit(solution)/shard_map/ppermute | solution.py:30
  862.1 17.4 collective-permute-done.19
  879.5 16.7 collective-permute-done.20
  925.1 18.4 collective-permute-start.14
  1035.5 16.2 add_add_fusion
  1085.0 19.6 collective-permute-start.42
  1111.8 29.7 %collective-permute-done.42 = bf16[1024,384]{1,0:T(8,128)(2,1)S(1)} collective-permute-done((bf16[1024,384]{1,0:T(8,128)(2,1)S(1)}, bf16[1024,384]{1,0:T(8,128)(2,1)S(1)}, u32[]{:S(2)}, u32[]{:S(2)}) %collective-permute-start.42) | collective-permute-done | bytes 786464 | tf_op jit(solution)/shard_map/ppermute | solution.py:30
  1152.3 59.0 %collective-permute-done.43 = bf16[1024,384]{1,0:T(8,128)(2,1)S(1)} collective-permute-done((bf16[1024,384]{1,0:T(8,128)(2,1)S(1)}, bf16[1024,384]{1,0:T(8,128)(2,1)S(1)}, u32[]{:S(2)}, u32[]{:S(2)}) %collective-permute-start.43) | collective-permute-done | bytes 786464 | tf_op jit(solution)/shard_map/ppermute | solution.py:30
  1211.4 36.7 %collective-permute-start.25 = (bf16[1024,384]{1,0:T(8,128)(2,1)S(1)}, bf16[1024,384]{1,0:T(8,128)(2,1)S(1)}, u32[]{:S(2)}, u32[]{:S(2)}) collective-permute-start(bf16[1024,384]{1,0:T(8,128)(2,1)S(1)} %get-tuple-element.119), channel_id=1, source_target_pairs={{0,2},{1,3},{2,0},{3,1},{4,6},{5,7},{6,4},{7,5},{8,10},{9,11},{10,... | collective-permute-start | bytes 2359304 | tf_op jit(solution)/shard_map/ppermute | solution.py:30
  1262.5 48.7 %collective-permute-done.46 = bf16[1024,384]{1,0:T(8,128)(2,1)S(1)} collective-permute-done((bf16[1024,384]{1,0:T(8,128)(2,1)S(1)}, bf16[1024,384]{1,0:T(8,128)(2,1)S(1)}, u32[]{:S(2)}, u32[]{:S(2)}) %collective-permute-start.46) | collective-permute-done | bytes 786464 | tf_op jit(solution)/shard_map/ppermute | solution.py:30
  1313.3 17.8 collective-permute-start.40
  1331.2 31.1 %collective-permute-start.41 = (bf16[1024,384]{1,0:T(8,128)(2,1)S(1)}, bf16[1024,384]{1,0:T(8,128)(2,1)S(1)}, u32[]{:S(2)}, u32[]{:S(2)}) collective-permute-start(bf16[1024,384]{1,0:T(8,128)(2,1)S(1)} %get-tuple-element.90), channel_id=1, source_target_pairs={{0,1},{1,2},{2,3},{3,0},{4,5},{5,6},{6,7},{7,4},{8,9},{9,10},{10,1... | collective-permute-start | bytes 2359304 | tf_op jit(solution)/shard_map/ppermute | solution.py:30
  1362.5 16.1 collective-permute-done.25
  1381.1 29.6 %collective-permute-done.40 = bf16[1024,384]{1,0:T(8,128)(2,1)S(1)} collective-permute-done((bf16[1024,384]{1,0:T(8,128)(2,1)S(1)}, bf16[1024,384]{1,0:T(8,128)(2,1)S(1)}, u32[]{:S(2)}, u32[]{:S(2)}) %collective-permute-start.40) | collective-permute-done | bytes 786464 | tf_op jit(solution)/shard_map/ppermute | solution.py:30
  1570.4 23.2 %collective-permute-start.34 = (bf16[1024,384]{1,0:T(8,128)(2,1)S(1)}, bf16[1024,384]{1,0:T(8,128)(2,1)S(1)}, u32[]{:S(2)}, u32[]{:S(2)}) collective-permute-start(bf16[1024,384]{1,0:T(8,128)(2,1)S(1)} %get-tuple-element.111), channel_id=1, source_target_pairs={{0,2},{1,3},{2,0},{3,1},{4,6},{5,7},{6,4},{7,5},{8,10},{9,11},{10,... | collective-permute-start | bytes 2359304 | tf_op jit(solution)/shard_map/ppermute | solution.py:30
  1611.7 47.9 %collective-permute-done.31 = bf16[1024,384]{1,0:T(8,128)(2,1)} collective-permute-done((bf16[1024,384]{1,0:T(8,128)(2,1)}, bf16[1024,384]{1,0:T(8,128)(2,1)}, u32[]{:S(2)}, u32[]{:S(2)}) %collective-permute-start.31) | collective-permute-done | bytes 786464 | tf_op jit(solution)/shard_map/ppermute | solution.py:30
  1679.0 48.0 %collective-permute-done.34 = bf16[1024,384]{1,0:T(8,128)(2,1)S(1)} collective-permute-done((bf16[1024,384]{1,0:T(8,128)(2,1)S(1)}, bf16[1024,384]{1,0:T(8,128)(2,1)S(1)}, u32[]{:S(2)}, u32[]{:S(2)}) %collective-permute-start.34) | collective-permute-done | bytes 786464 | tf_op jit(solution)/shard_map/ppermute | solution.py:30
  1729.9 30.5 %collective-permute-done.37 = bf16[1024,384]{1,0:T(8,128)(2,1)S(1)} collective-permute-done((bf16[1024,384]{1,0:T(8,128)(2,1)S(1)}, bf16[1024,384]{1,0:T(8,128)(2,1)S(1)}, u32[]{:S(2)}, u32[]{:S(2)}) %collective-permute-start.37) | collective-permute-done | bytes 786464 | tf_op jit(solution)/shard_map/ppermute | solution.py:30
  1767.0 16.1 fusion.64
  1829.7 31.8 %bitcast_multiply_fusion = (f32[256,64,384]{0,2,1:T(8,128)}, f32[64,384,256]{2,1,0:T(8,128)}) fusion(f32[64,384,256]{2,1,0:T(8,128)} %fusion.14, bf16[256,256,1]{1,0,2:T(8,128)(2,1)S(1)} %bitcast.370, bf16[64,64,384]{0,2,1:T(8,128)(2,1)} %copy.287, bf16[64,64,384]{0,2,1:T(8,128)(2,1)} %copy.286, bf16[64,64,384]{0,2,1:T(8,128)(2,1)} %copy.285, ...), kind=kOutput, calls=%fused_computation.4 | convolution fusion | flops 3277848576 | bytes 88211456 | tf_op jit(solution)/shard_map/gec,fg->fec/dot_general | solution.py:229
  1861.4 18.2 convert_bitcast_fusion
  1896.7 16.2 fusion.96
  1916.4 18.2 all-to-all-done.9
  1939.0 16.2 fusion.128
  1958.8 18.1 all-to-all-done.10
  1981.4 16.2 fusion.160
  2001.1 18.2 all-to-all-done.11
  2039.7 25.0 %copy.312 = f32[256,64,384]{2,1,0:T(8,128)} copy(f32[256,64,384]{0,2,1:T(8,128)} %get-tuple-element.171) | data formatting | bytes 50331648
  2150.4 72.4 %pad_maximum_fusion.1 = bf16[16384,384]{1,0:T(8,128)(2,1)} fusion(bf16[4096,384]{1,0:T(8,128)(2,1)S(1)} %fusion.298, bf16[4096,384]{1,0:T(8,128)(2,1)S(1)} %fusion.299, bf16[4096,384]{1,0:T(8,128)(2,1)S(1)} %copy-done.15, bf16[4096,384]{1,0:T(8,128)(2,1)S(1)} %copy-done.14), kind=kLoop, calls=%fused_computation.20 | loop fusion | flops 50331648 | bytes 25165824 | tf_op jit(solution)/shard_map/concatenate | solution.py:253
  (415 shorter events, 865.9 us)
Async XLA Ops:
  51.5 272.1 %all-to-all-start = ((bf16[32,512,384]{2,0,1:T(8,128)(2,1)}), bf16[32,512,384]{2,0,1:T(8,128)(2,1)}, u32[]{:S(2)}, u32[]{:S(2)}) async-start(bf16[32,512,384]{2,0,1:T(8,128)(2,1)} %copy.242), calls=%async_computation | async-start | bytes 25165824 | tf_op jit(solution)/shard_map/all_to_all | solution.py:152
  68.2 100.9 %collective-permute-start.2 = (bf16[1024,384]{1,0:T(8,128)(2,1)S(1)}, bf16[1024,384]{1,0:T(8,128)(2,1)}, u32[]{:S(2)}, u32[]{:S(2)}) collective-permute-start(bf16[1024,384]{1,0:T(8,128)(2,1)S(1)} %get-tuple-element.151), channel_id=1, source_target_pairs={{0,3},{1,0},{2,1},{3,2},{4,7},{5,4},{6,5},{7,6},{8,11},{9,8},{10,9... | collective-permute-start | bytes 2359304 | tf_op jit(solution)/shard_map/ppermute | solution.py:30
  71.0 102.1 %collective-permute-start.3 = (bf16[1024,384]{1,0:T(8,128)(2,1)S(1)}, bf16[1024,384]{1,0:T(8,128)(2,1)}, u32[]{:S(2)}, u32[]{:S(2)}) collective-permute-start(bf16[1024,384]{1,0:T(8,128)(2,1)S(1)} %get-tuple-element.149), channel_id=1, source_target_pairs={{0,1},{1,2},{2,3},{3,0},{4,5},{5,6},{6,7},{7,4},{8,9},{9,10},{10,1... | collective-permute-start | bytes 2359304 | tf_op jit(solution)/shard_map/ppermute | solution.py:30
  71.7 149.1 %collective-permute-start.4 = (bf16[1024,384]{1,0:T(8,128)(2,1)}, bf16[1024,384]{1,0:T(8,128)(2,1)}, u32[]{:S(2)}, u32[]{:S(2)}) collective-permute-start(bf16[1024,384]{1,0:T(8,128)(2,1)} %get-tuple-element.148), channel_id=1, source_target_pairs={{0,2},{1,3},{2,0},{3,1},{4,6},{5,7},{6,4},{7,5},{8,10},{9,11},{10,... | collective-permute-start | bytes 2359304 | tf_op jit(solution)/shard_map/ppermute | solution.py:30
  86.1 155.2 %collective-permute-start.5 = (bf16[1024,384]{1,0:T(8,128)(2,1)}, bf16[1024,384]{1,0:T(8,128)(2,1)}, u32[]{:S(2)}, u32[]{:S(2)}) collective-permute-start(bf16[1024,384]{1,0:T(8,128)(2,1)} %get-tuple-element.147), channel_id=1, source_target_pairs={{0,3},{1,0},{2,1},{3,2},{4,7},{5,4},{6,5},{7,6},{8,11},{9,8},{10,9... | collective-permute-start | bytes 2359304 | tf_op jit(solution)/shard_map/ppermute | solution.py:30
  119.9 145.1 %collective-permute-start.6 = (bf16[1024,384]{1,0:T(8,128)(2,1)}, bf16[1024,384]{1,0:T(8,128)(2,1)}, u32[]{:S(2)}, u32[]{:S(2)}) collective-permute-start(bf16[1024,384]{1,0:T(8,128)(2,1)} %get-tuple-element.145), channel_id=1, source_target_pairs={{0,1},{1,2},{2,3},{3,0},{4,5},{5,6},{6,7},{7,4},{8,9},{9,10},{10,1... | collective-permute-start | bytes 2359304 | tf_op jit(solution)/shard_map/ppermute | solution.py:30
  169.1 124.4 %collective-permute-start.7 = (bf16[1024,384]{1,0:T(8,128)(2,1)}, bf16[1024,384]{1,0:T(8,128)(2,1)}, u32[]{:S(2)}, u32[]{:S(2)}) collective-permute-start(bf16[1024,384]{1,0:T(8,128)(2,1)} %get-tuple-element.144), channel_id=1, source_target_pairs={{0,2},{1,3},{2,0},{3,1},{4,6},{5,7},{6,4},{7,5},{8,10},{9,11},{10,... | collective-permute-start | bytes 2359304 | tf_op jit(solution)/shard_map/ppermute | solution.py:30
  173.1 120.4 %collective-permute-start.8 = (bf16[1024,384]{1,0:T(8,128)(2,1)}, bf16[1024,384]{1,0:T(8,128)(2,1)}, u32[]{:S(2)}, u32[]{:S(2)}) collective-permute-start(bf16[1024,384]{1,0:T(8,128)(2,1)} %get-tuple-element.143), channel_id=1, source_target_pairs={{0,3},{1,0},{2,1},{3,2},{4,7},{5,4},{6,5},{7,6},{8,11},{9,8},{10,9... | collective-permute-start | bytes 2359304 | tf_op jit(solution)/shard_map/ppermute | solution.py:30
  220.7 101.1 %collective-permute-start.10 = (bf16[1024,384]{1,0:T(8,128)(2,1)}, bf16[1024,384]{1,0:T(8,128)(2,1)S(1)}, u32[]{:S(2)}, u32[]{:S(2)}) collective-permute-start(bf16[1024,384]{1,0:T(8,128)(2,1)} %get-tuple-element.140), channel_id=1, source_target_pairs={{0,2},{1,3},{2,0},{3,1},{4,6},{5,7},{6,4},{7,5},{8,10},{9,11},{10,... | collective-permute-start | bytes 2359304 | tf_op jit(solution)/shard_map/ppermute | solution.py:30
  241.3 80.5 %collective-permute-start.11 = (bf16[1024,384]{1,0:T(8,128)(2,1)}, bf16[1024,384]{1,0:T(8,128)(2,1)S(1)}, u32[]{:S(2)}, u32[]{:S(2)}) collective-permute-start(bf16[1024,384]{1,0:T(8,128)(2,1)} %get-tuple-element.139), channel_id=1, source_target_pairs={{0,3},{1,0},{2,1},{3,2},{4,7},{5,4},{6,5},{7,6},{8,11},{9,8},{10,9... | collective-permute-start | bytes 2359304 | tf_op jit(solution)/shard_map/ppermute | solution.py:30
  549.5 80.3 %all-to-all-start.4 = ((bf16[64,64,384]{2,1,0:T(8,128)(2,1)}), bf16[64,64,384]{2,1,0:T(8,128)(2,1)}, u32[]{:S(2)}, u32[]{:S(2)}) async-start(bf16[64,64,384]{2,1,0:T(8,128)(2,1)} %copy.264), calls=%async_computation.4 | async-start | bytes 6291456 | tf_op jit(solution)/shard_map/all_to_all | solution.py:164
  554.0 1510.7 %reduce-scatter.9.cloned.1.call-start = ((), (), s32[]{:S(2)}) async-start(), calls=%async_computation.19 | async-start | bytes 2949120 | tf_op jit(solution)/shard_map/reduce_scatter | solution.py:102
  697.2 278.6 %collective-permute-start.12 = (bf16[1024,384]{0,1:T(8,128)(2,1)S(1)}, bf16[1024,384]{0,1:T(8,128)(2,1)S(1)}, u32[]{:S(2)}, u32[]{:S(2)}) collective-permute-start(bf16[1024,384]{0,1:T(8,128)(2,1)S(1)} %get-tuple-element.137), channel_id=1, source_target_pairs={{0,1},{1,2},{2,3},{3,0},{4,5},{5,6},{6,7},{7,4},{8,9},{9,10},{10,1... | collective-permute-start | bytes 2359304 | tf_op jit(solution)/shard_map/ppermute | solution.py:30
  697.9 277.9 %collective-permute-start.13 = (bf16[1024,384]{0,1:T(8,128)(2,1)S(1)}, bf16[1024,384]{0,1:T(8,128)(2,1)S(1)}, u32[]{:S(2)}, u32[]{:S(2)}) collective-permute-start(bf16[1024,384]{0,1:T(8,128)(2,1)S(1)} %get-tuple-element.136), channel_id=1, source_target_pairs={{0,2},{1,3},{2,0},{3,1},{4,6},{5,7},{6,4},{7,5},{8,10},{9,11},{10,... | collective-permute-start | bytes 2359304 | tf_op jit(solution)/shard_map/ppermute | solution.py:30
  711.3 84.3 %collective-permute-start.18 = (bf16[1024,384]{0,1:T(8,128)(2,1)S(1)}, bf16[1024,384]{0,1:T(8,128)(2,1)S(1)}, u32[]{:S(2)}, u32[]{:S(2)}) collective-permute-start(bf16[1024,384]{0,1:T(8,128)(2,1)S(1)} %get-tuple-element.129), channel_id=1, source_target_pairs={{0,1},{1,2},{2,3},{3,0},{4,5},{5,6},{6,7},{7,4},{8,9},{9,10},{10,1... | collective-permute-start | bytes 2359304 | tf_op jit(solution)/shard_map/ppermute | solution.py:30
  745.0 134.6 %collective-permute-start.19 = (bf16[1024,384]{0,1:T(8,128)(2,1)S(1)}, bf16[1024,384]{0,1:T(8,128)(2,1)S(1)}, u32[]{:S(2)}, u32[]{:S(2)}) collective-permute-start(bf16[1024,384]{0,1:T(8,128)(2,1)S(1)} %get-tuple-element.128), channel_id=1, source_target_pairs={{0,2},{1,3},{2,0},{3,1},{4,6},{5,7},{6,4},{7,5},{8,10},{9,11},{10,... | collective-permute-start | bytes 2359304 | tf_op jit(solution)/shard_map/ppermute | solution.py:30
  745.0 151.3 %collective-permute-start.20 = (bf16[1024,384]{0,1:T(8,128)(2,1)S(1)}, bf16[1024,384]{0,1:T(8,128)(2,1)S(1)}, u32[]{:S(2)}, u32[]{:S(2)}) collective-permute-start(bf16[1024,384]{0,1:T(8,128)(2,1)S(1)} %get-tuple-element.127), channel_id=1, source_target_pairs={{0,3},{1,0},{2,1},{3,2},{4,7},{5,4},{6,5},{7,6},{8,11},{9,8},{10,9... | collective-permute-start | bytes 2359304 | tf_op jit(solution)/shard_map/ppermute | solution.py:30
  795.6 129.5 %collective-permute-start.21 = (bf16[1024,384]{0,1:T(8,128)(2,1)S(1)}, bf16[1024,384]{0,1:T(8,128)(2,1)S(1)}, u32[]{:S(2)}, u32[]{:S(2)}) collective-permute-start(bf16[1024,384]{0,1:T(8,128)(2,1)S(1)} %get-tuple-element.125), channel_id=1, source_target_pairs={{0,1},{1,2},{2,3},{3,0},{4,5},{5,6},{6,7},{7,4},{8,9},{9,10},{10,1... | collective-permute-start | bytes 2359304 | tf_op jit(solution)/shard_map/ppermute | solution.py:30
  879.5 63.9 %collective-permute-start.22 = (bf16[1024,384]{0,1:T(8,128)(2,1)S(1)}, bf16[1024,384]{0,1:T(8,128)(2,1)S(1)}, u32[]{:S(2)}, u32[]{:S(2)}) collective-permute-start(bf16[1024,384]{0,1:T(8,128)(2,1)S(1)} %get-tuple-element.124), channel_id=1, source_target_pairs={{0,2},{1,3},{2,0},{3,1},{4,6},{5,7},{6,4},{7,5},{8,10},{9,11},{10,... | collective-permute-start | bytes 2359304 | tf_op jit(solution)/shard_map/ppermute | solution.py:30
  1104.5 106.7 %collective-permute-start.43 = (bf16[1024,384]{1,0:T(8,128)(2,1)S(1)}, bf16[1024,384]{1,0:T(8,128)(2,1)S(1)}, u32[]{:S(2)}, u32[]{:S(2)}) collective-permute-start(bf16[1024,384]{1,0:T(8,128)(2,1)S(1)} %get-tuple-element.95), channel_id=1, source_target_pairs={{0,2},{1,3},{2,0},{3,1},{4,6},{5,7},{6,4},{7,5},{8,10},{9,11},{10,... | collective-permute-start | bytes 2359304 | tf_op jit(solution)/shard_map/ppermute | solution.py:30
  1104.6 106.9 %collective-permute-start.44 = (bf16[1024,384]{1,0:T(8,128)(2,1)S(1)}, bf16[1024,384]{1,0:T(8,128)(2,1)S(1)}, u32[]{:S(2)}, u32[]{:S(2)}) collective-permute-start(bf16[1024,384]{1,0:T(8,128)(2,1)S(1)} %get-tuple-element.94), channel_id=1, source_target_pairs={{0,1},{1,2},{2,3},{3,0},{4,5},{5,6},{6,7},{7,4},{8,9},{9,10},{10,1... | collective-permute-start | bytes 2359304 | tf_op jit(solution)/shard_map/ppermute | solution.py:30
  1105.9 142.4 %collective-permute-start.45 = (bf16[1024,384]{1,0:T(8,128)(2,1)S(1)}, bf16[1024,384]{1,0:T(8,128)(2,1)S(1)}, u32[]{:S(2)}, u32[]{:S(2)}) collective-permute-start(bf16[1024,384]{1,0:T(8,128)(2,1)S(1)} %get-tuple-element.100), channel_id=1, source_target_pairs={{0,3},{1,0},{2,1},{3,2},{4,7},{5,4},{6,5},{7,6},{8,11},{9,8},{10,9... | collective-permute-start | bytes 2359304 | tf_op jit(solution)/shard_map/ppermute | solution.py:30
  1109.3 201.9 %collective-permute-start.46 = (bf16[1024,384]{1,0:T(8,128)(2,1)S(1)}, bf16[1024,384]{1,0:T(8,128)(2,1)S(1)}, u32[]{:S(2)}, u32[]{:S(2)}) collective-permute-start(bf16[1024,384]{1,0:T(8,128)(2,1)S(1)} %get-tuple-element.99), channel_id=1, source_target_pairs={{0,2},{1,3},{2,0},{3,1},{4,6},{5,7},{6,4},{7,5},{8,10},{9,11},{10,... | collective-permute-start | bytes 2359304 | tf_op jit(solution)/shard_map/ppermute | solution.py:30
  1141.5 171.7 %collective-permute-start.47 = (bf16[1024,384]{1,0:T(8,128)(2,1)S(1)}, bf16[1024,384]{1,0:T(8,128)(2,1)S(1)}, u32[]{:S(2)}, u32[]{:S(2)}) collective-permute-start(bf16[1024,384]{1,0:T(8,128)(2,1)S(1)} %get-tuple-element.98), channel_id=1, source_target_pairs={{0,1},{1,2},{2,3},{3,0},{4,5},{5,6},{6,7},{7,4},{8,9},{9,10},{10,1... | collective-permute-start | bytes 2359304 | tf_op jit(solution)/shard_map/ppermute | solution.py:30
  1211.3 119.9 %collective-permute-start.24 = (bf16[1024,384]{1,0:T(8,128)(2,1)S(1)}, bf16[1024,384]{1,0:T(8,128)(2,1)S(1)}, u32[]{:S(2)}, u32[]{:S(2)}) collective-permute-start(bf16[1024,384]{1,0:T(8,128)(2,1)S(1)} %get-tuple-element.120), channel_id=1, source_target_pairs={{0,3},{1,0},{2,1},{3,2},{4,7},{5,4},{6,5},{7,6},{8,11},{9,8},{10,9... | collective-permute-start | bytes 2359304 | tf_op jit(solution)/shard_map/ppermute | solution.py:30
  1211.4 167.2 %collective-permute-start.25 = (bf16[1024,384]{1,0:T(8,128)(2,1)S(1)}, bf16[1024,384]{1,0:T(8,128)(2,1)S(1)}, u32[]{:S(2)}, u32[]{:S(2)}) collective-permute-start(bf16[1024,384]{1,0:T(8,128)(2,1)S(1)} %get-tuple-element.119), channel_id=1, source_target_pairs={{0,2},{1,3},{2,0},{3,1},{4,6},{5,7},{6,4},{7,5},{8,10},{9,11},{10,... | collective-permute-start | bytes 2359304 | tf_op jit(solution)/shard_map/ppermute | solution.py:30
  1248.3 132.4 %collective-permute-start.26 = (bf16[1024,384]{1,0:T(8,128)(2,1)S(1)}, bf16[1024,384]{1,0:T(8,128)(2,1)S(1)}, u32[]{:S(2)}, u32[]{:S(2)}) collective-permute-start(bf16[1024,384]{1,0:T(8,128)(2,1)S(1)} %get-tuple-element.118), channel_id=1, source_target_pairs={{0,1},{1,2},{2,3},{3,0},{4,5},{5,6},{6,7},{7,4},{8,9},{9,10},{10,1... | collective-permute-start | bytes 2359304 | tf_op jit(solution)/shard_map/ppermute | solution.py:30
  1311.2 69.6 %collective-permute-start.39 = (bf16[1024,384]{1,0:T(8,128)(2,1)S(1)}, bf16[1024,384]{1,0:T(8,128)(2,1)S(1)}, u32[]{:S(2)}, u32[]{:S(2)}) collective-permute-start(bf16[1024,384]{1,0:T(8,128)(2,1)S(1)} %get-tuple-element.92), channel_id=1, source_target_pairs={{0,3},{1,0},{2,1},{3,2},{4,7},{5,4},{6,5},{7,6},{8,11},{9,8},{10,9... | collective-permute-start | bytes 2359304 | tf_op jit(solution)/shard_map/ppermute | solution.py:30
  1313.3 97.4 %collective-permute-start.40 = (bf16[1024,384]{1,0:T(8,128)(2,1)S(1)}, bf16[1024,384]{1,0:T(8,128)(2,1)S(1)}, u32[]{:S(2)}, u32[]{:S(2)}) collective-permute-start(bf16[1024,384]{1,0:T(8,128)(2,1)S(1)} %get-tuple-element.91), channel_id=1, source_target_pairs={{0,2},{1,3},{2,0},{3,1},{4,6},{5,7},{6,4},{7,5},{8,10},{9,11},{10,... | collective-permute-start | bytes 2359304 | tf_op jit(solution)/shard_map/ppermute | solution.py:30
  1331.2 81.5 %collective-permute-start.41 = (bf16[1024,384]{1,0:T(8,128)(2,1)S(1)}, bf16[1024,384]{1,0:T(8,128)(2,1)S(1)}, u32[]{:S(2)}, u32[]{:S(2)}) collective-permute-start(bf16[1024,384]{1,0:T(8,128)(2,1)S(1)} %get-tuple-element.90), channel_id=1, source_target_pairs={{0,1},{1,2},{2,3},{3,0},{4,5},{5,6},{6,7},{7,4},{8,9},{9,10},{10,1... | collective-permute-start | bytes 2359304 | tf_op jit(solution)/shard_map/ppermute | solution.py:30
  1434.3 60.6 %all-to-all-start.5 = ((bf16[8,512,384]{2,0,1:T(8,128)(2,1)}), bf16[8,512,384]{2,0,1:T(8,128)(2,1)}, u32[]{:S(2)}, u32[]{:S(2)}) async-start(bf16[8,512,384]{2,0,1:T(8,128)(2,1)} %copy.269), calls=%async_computation.5 | async-start | bytes 6291456 | tf_op jit(solution)/shard_map/all_to_all | solution.py:217
  1487.6 71.9 %collective-permute-start.27 = (bf16[1024,384]{1,0:T(8,128)(2,1)}, bf16[1024,384]{1,0:T(8,128)(2,1)}, u32[]{:S(2)}, u32[]{:S(2)}) collective-permute-start(bf16[1024,384]{1,0:T(8,128)(2,1)} %get-tuple-element.104), channel_id=1, source_target_pairs={{0,3},{1,0},{2,1},{3,2},{4,7},{5,4},{6,5},{7,6},{8,11},{9,8},{10,9... | collective-permute-start | bytes 2359304 | tf_op jit(solution)/shard_map/ppermute | solution.py:30
  1487.6 71.9 %collective-permute-start.28 = (bf16[1024,384]{1,0:T(8,128)(2,1)}, bf16[1024,384]{1,0:T(8,128)(2,1)}, u32[]{:S(2)}, u32[]{:S(2)}) collective-permute-start(bf16[1024,384]{1,0:T(8,128)(2,1)} %get-tuple-element.103), channel_id=1, source_target_pairs={{0,2},{1,3},{2,0},{3,1},{4,6},{5,7},{6,4},{7,5},{8,10},{9,11},{10,... | collective-permute-start | bytes 2359304 | tf_op jit(solution)/shard_map/ppermute | solution.py:30
  1489.2 81.2 %collective-permute-start.29 = (bf16[1024,384]{1,0:T(8,128)(2,1)}, bf16[1024,384]{1,0:T(8,128)(2,1)}, u32[]{:S(2)}, u32[]{:S(2)}) collective-permute-start(bf16[1024,384]{1,0:T(8,128)(2,1)} %get-tuple-element.102), channel_id=1, source_target_pairs={{0,1},{1,2},{2,3},{3,0},{4,5},{5,6},{6,7},{7,4},{8,9},{9,10},{10,1... | collective-permute-start | bytes 2359304 | tf_op jit(solution)/shard_map/ppermute | solution.py:30
  1499.4 723.4 %reduce-scatter.13.cloned.1.call-start = ((), (), s32[]{:S(2)}) async-start(), calls=%async_computation.21 | async-start | bytes 663552
  1505.0 90.6 %collective-permute-start.30 = (bf16[1024,384]{1,0:T(8,128)(2,1)}, bf16[1024,384]{1,0:T(8,128)(2,1)}, u32[]{:S(2)}, u32[]{:S(2)}) collective-permute-start(bf16[1024,384]{1,0:T(8,128)(2,1)} %get-tuple-element.108), channel_id=1, source_target_pairs={{0,3},{1,0},{2,1},{3,2},{4,7},{5,4},{6,5},{7,6},{8,11},{9,8},{10,9... | collective-permute-start | bytes 2359304 | tf_op jit(solution)/shard_map/ppermute | solution.py:30
  1507.2 152.5 %collective-permute-start.31 = (bf16[1024,384]{1,0:T(8,128)(2,1)}, bf16[1024,384]{1,0:T(8,128)(2,1)}, u32[]{:S(2)}, u32[]{:S(2)}) collective-permute-start(bf16[1024,384]{1,0:T(8,128)(2,1)} %get-tuple-element.107), channel_id=1, source_target_pairs={{0,2},{1,3},{2,0},{3,1},{4,6},{5,7},{6,4},{7,5},{8,10},{9,11},{10,... | collective-permute-start | bytes 2359304 | tf_op jit(solution)/shard_map/ppermute | solution.py:30
  1538.9 223.5 %all-to-all-start.7 = ((bf16[8,512,384]{2,0,1:T(8,128)(2,1)}), bf16[8,512,384]{2,0,1:T(8,128)(2,1)}, u32[]{:S(2)}, u32[]{:S(2)}) async-start(bf16[8,512,384]{2,0,1:T(8,128)(2,1)} %copy.277), calls=%async_computation.7 | async-start | bytes 6291456 | tf_op jit(solution)/shard_map/all_to_all | solution.py:217
  1543.4 679.4 %reduce-scatter.7.cloned.1.call-start = ((), (), s32[]{:S(2)}) async-start(), calls=%async_computation.18 | async-start | bytes 663552 | tf_op jit(solution)/shard_map/reduce_scatter | solution.py:260
  1559.4 102.3 %collective-permute-start.32 = (bf16[1024,384]{1,0:T(8,128)(2,1)S(1)}, bf16[1024,384]{1,0:T(8,128)(2,1)S(1)}, u32[]{:S(2)}, u32[]{:S(2)}) collective-permute-start(bf16[1024,384]{1,0:T(8,128)(2,1)S(1)} %copy-done.41), channel_id=1, source_target_pairs={{0,1},{1,2},{2,3},{3,0},{4,5},{5,6},{6,7},{7,4},{8,9},{9,10},{10,1... | collective-permute-start | bytes 2359304 | tf_op jit(solution)/shard_map/ppermute | solution.py:30
  1559.4 104.4 %collective-permute-start.33 = (bf16[1024,384]{1,0:T(8,128)(2,1)}, bf16[1024,384]{1,0:T(8,128)(2,1)S(1)}, u32[]{:S(2)}, u32[]{:S(2)}) collective-permute-start(bf16[1024,384]{1,0:T(8,128)(2,1)} %get-tuple-element.112), channel_id=1, source_target_pairs={{0,3},{1,0},{2,1},{3,2},{4,7},{5,4},{6,5},{7,6},{8,11},{9,8},{10,9... | collective-permute-start | bytes 2359304 | tf_op jit(solution)/shard_map/ppermute | solution.py:30
  1570.4 156.6 %collective-permute-start.34 = (bf16[1024,384]{1,0:T(8,128)(2,1)S(1)}, bf16[1024,384]{1,0:T(8,128)(2,1)S(1)}, u32[]{:S(2)}, u32[]{:S(2)}) collective-permute-start(bf16[1024,384]{1,0:T(8,128)(2,1)S(1)} %get-tuple-element.111), channel_id=1, source_target_pairs={{0,2},{1,3},{2,0},{3,1},{4,6},{5,7},{6,4},{7,5},{8,10},{9,11},{10,... | collective-permute-start | bytes 2359304 | tf_op jit(solution)/shard_map/ppermute | solution.py:30
  1595.7 132.3 %collective-permute-start.35 = (bf16[1024,384]{1,0:T(8,128)(2,1)S(1)}, bf16[1024,384]{1,0:T(8,128)(2,1)S(1)}, u32[]{:S(2)}, u32[]{:S(2)}) collective-permute-start(bf16[1024,384]{1,0:T(8,128)(2,1)S(1)} %get-tuple-element.110), channel_id=1, source_target_pairs={{0,1},{1,2},{2,3},{3,0},{4,5},{5,6},{6,7},{7,4},{8,9},{9,10},{10,1... | collective-permute-start | bytes 2359304 | tf_op jit(solution)/shard_map/ppermute | solution.py:30
  1659.6 69.3 %collective-permute-start.36 = (bf16[1024,384]{1,0:T(8,128)(2,1)S(1)}, bf16[1024,384]{1,0:T(8,128)(2,1)S(1)}, u32[]{:S(2)}, u32[]{:S(2)}) collective-permute-start(bf16[1024,384]{1,0:T(8,128)(2,1)S(1)} %get-tuple-element.116), channel_id=1, source_target_pairs={{0,3},{1,0},{2,1},{3,2},{4,7},{5,4},{6,5},{7,6},{8,11},{9,8},{10,9... | collective-permute-start | bytes 2359304 | tf_op jit(solution)/shard_map/ppermute | solution.py:30
  1661.8 98.7 %collective-permute-start.37 = (bf16[1024,384]{1,0:T(8,128)(2,1)S(1)}, bf16[1024,384]{1,0:T(8,128)(2,1)S(1)}, u32[]{:S(2)}, u32[]{:S(2)}) collective-permute-start(bf16[1024,384]{1,0:T(8,128)(2,1)S(1)} %get-tuple-element.115), channel_id=1, source_target_pairs={{0,2},{1,3},{2,0},{3,1},{4,6},{5,7},{6,4},{7,5},{8,10},{9,11},{10,... | collective-permute-start | bytes 2359304 | tf_op jit(solution)/shard_map/ppermute | solution.py:30
  1663.9 97.5 %collective-permute-start.38 = (bf16[1024,384]{1,0:T(8,128)(2,1)S(1)}, bf16[1024,384]{1,0:T(8,128)(2,1)S(1)}, u32[]{:S(2)}, u32[]{:S(2)}) collective-permute-start(bf16[1024,384]{1,0:T(8,128)(2,1)S(1)} %get-tuple-element.114), channel_id=1, source_target_pairs={{0,1},{1,2},{2,3},{3,0},{4,5},{5,6},{6,7},{7,4},{8,9},{9,10},{10,1... | collective-permute-start | bytes 2359304 | tf_op jit(solution)/shard_map/ppermute | solution.py:30
  2019.3 89.6 %all-to-all-start.12 = ((bf16[64,64,384]{2,1,0:T(8,128)(2,1)}), bf16[64,64,384]{2,1,0:T(8,128)(2,1)}, u32[]{:S(2)}, u32[]{:S(2)}) async-start(bf16[64,64,384]{2,1,0:T(8,128)(2,1)} %copy.302), calls=%async_computation.12 | async-start | bytes 6291456 | tf_op jit(solution)/shard_map/all_to_all | solution.py:242
  2023.7 199.1 %reduce-scatter.11.cloned.1.call-start = ((), (), s32[]{:S(2)}) async-start(), calls=%async_computation.20 | async-start | bytes 663552 | tf_op jit(solution)/shard_map/reduce_scatter | solution.py:262
  (83 other events, 2881.4 us)
Sparse Core Ops, SparseCore 0:
  471.3 46.7 all-gather.1
  1082.4 119.3 reduce-scatter.8
  1507.3 36.9 reduce-scatter.12
  1549.1 35.7 reduce-scatter.6
  2068.2 32.9 reduce-scatter.10
